TPU v7x, 128 devices: a whole 4x4x4 slice. The times are simulated.
128 devices in a mesh: rep: 16 (over y, z_lo, core), shard: 8 (over z_hi, x).
Axes of the slice: x: 4, y: 4, z: 4 (z_hi: 2, z_lo: 2; z = z_hi * 2 + z_lo), core: 2. Of those that a mesh axis runs over, the one named last changes fastest.
Arguments:
- tokens: bfloat16 [24576, 1152], P(('rep', 'shard')), may hold values from -6 to 6
- lengths: int32 [16, 8], P('rep', 'shard'), may hold values from 128 to 192, as said below
- attn_gain: bfloat16 [1152], P('shard'), may hold values from 0.25 to 1.75
- w_query: bfloat16 [1152, 1024], P('shard'), may hold values from -0.1875 to 0.1875
- w_keyval: bfloat16 [1152, 512], P('shard'), may hold values from -0.1875 to 0.1875
- w_out: bfloat16 [1024, 1152], P('shard'), may hold values from -1.5 to 1.5
- mlp_gain: bfloat16 [1152], P('shard'), may hold values from 0.25 to 1.75
- w_gate: bfloat16 [1152, 6912], P('shard'), may hold values from -0.1875 to 0.1875
- w_up: bfloat16 [1152, 6912], P('shard'), may hold values from -0.1875 to 0.1875
- w_down: bfloat16 [6912, 1152], P('shard'), may hold values from -0.15625 to 0.15625
- cotangent: bfloat16 [24576, 1152], P(('rep', 'shard')), may hold values from -6 to 6
Outputs:
- outputs: bfloat16 [24576, 1152], P(('rep', 'shard'))
- grad_tokens: float32 [24576, 1152], P(('rep', 'shard'))
- grad_attn_gain: float32 [1152], P('shard')
- grad_w_query: float32 [1152, 1024], P('shard')
- grad_w_keyval: float32 [1152, 512], P('shard')
- grad_w_out: float32 [1024, 1152], P('shard')
- grad_mlp_gain: float32 [1152], P('shard')
- grad_w_gate: float32 [1152, 6912], P('shard')
- grad_w_up: float32 [1152, 6912], P('shard')
- grad_w_down: float32 [6912, 1152], P('shard')
Inputs may be any that keep to these rules, and one draw needn't show every extreme that they name: lengths[r, s] counts the live slots at the start of the 192 slots of shard index s in sequence r; in every sequence one device has all 192 live and another has exactly 128.
All inputs are finite; a program needn't handle non-finite values.
Results may differ from a plain program's by a relative error of at most 0.025.
Values may be sent and summed in bfloat16 or wider, within the bound.
A program may use at most 256 MiB of HBM per device.

v0:
```python
import jax
import jax.numpy as jnp
from jax import lax
from jax.sharding import PartitionSpec as P

WINDOW = 512


EPSILON = 1e-06
MASKED = -1e30


def matmul(former, latter):
    return jnp.dot(former, latter, preferred_element_type=jnp.float32)


def lead_product(former, latter):
    return lax.dot_general(
        former, latter, (((0,), (0,)), ((), ())), preferred_element_type=jnp.float32
    )


def trail_product(former, latter):
    return lax.dot_general(
        former, latter, (((1,), (1,)), ((), ())), preferred_element_type=jnp.float32
    )


def rotate(vectors, cosine, sine_part):
    half_size = vectors.shape[-1] // 2
    first_half = vectors[..., :half_size]
    second_half = vectors[..., half_size:]
    return jnp.concatenate(
        [
            first_half * cosine - second_half * sine_part,
            second_half * cosine + first_half * sine_part,
        ],
        axis=-1,
    )


def norm_back(grad_normed, scaled, inverse, gain_values):
    grad_scaled = grad_normed * gain_values
    return inverse * (grad_scaled - scaled * jnp.mean(grad_scaled * scaled, axis=1, keepdims=True))


def on_device(
    tokens, lengths, attn_gain, w_query, w_keyval, w_out, mlp_gain, w_gate, w_up, w_down, cotangent
):
    row_count = tokens.shape[0]
    head_size = w_keyval.shape[1] // 2
    heads_all = w_query.shape[1]
    head_count = heads_all // head_size
    shards = lax.axis_size("shard")
    scaling = head_size ** (-0.5)
    live_all = lax.all_gather(lengths, "shard", axis=1, tiled=True)[0]
    starts = jnp.cumsum(live_all) - live_all
    is_mine = jnp.arange(shards) == lax.axis_index("shard")
    live_count = jnp.sum(jnp.where(is_mine, live_all, 0))
    offset = jnp.sum(jnp.where(is_mine, starts, 0))
    within = jnp.arange(row_count, dtype=jnp.int32)
    query_pos = offset + within
    keep_mask = (within < live_count).astype(jnp.float32)[:, None]
    key_within = jnp.tile(within, shards)
    key_pos = jnp.repeat(starts, row_count, total_repeat_length=shards * row_count) + key_within
    key_live = key_within < jnp.repeat(live_all, row_count, total_repeat_length=shards * row_count)
    allowed = (
        key_live[None, :]
        & (key_pos[None, :] <= query_pos[:, None])
        & (query_pos[:, None] - key_pos[None, :] < WINDOW)
    )
    half_size = head_size // 2
    frequency = 10000.0 ** (-2.0 * jnp.arange(half_size, dtype=jnp.float32) / head_size)
    angles = query_pos.astype(jnp.float32)[:, None] * frequency[None, :]
    cosine = jnp.cos(angles)
    sine_part = jnp.sin(angles)
    heads_cos = cosine[:, None, :]
    heads_sin = sine_part[:, None, :]
    inputs = tokens.astype(jnp.float32)
    inverse1 = lax.rsqrt(jnp.mean(inputs * inputs, axis=1, keepdims=True) + EPSILON)
    scaled1 = inputs * inverse1
    gain1, query_full, keyval_full, out_full = (
        lax.all_gather(attn_gain, "shard", axis=0, tiled=True),
        lax.all_gather(w_query, "shard", axis=0, tiled=True),
        lax.all_gather(w_keyval, "shard", axis=0, tiled=True),
        lax.all_gather(w_out, "shard", axis=0, tiled=True),
    )
    normed1 = (scaled1 * gain1.astype(jnp.float32)).astype(jnp.bfloat16)
    queries = (
        rotate(
            matmul(normed1, query_full).reshape(row_count, head_count, head_size),
            heads_cos,
            heads_sin,
        )
        * scaling
    ).astype(jnp.bfloat16)
    projected = matmul(normed1, keyval_full)
    own_keys = rotate(projected[:, :head_size], cosine, sine_part).astype(jnp.bfloat16)
    own_values = projected[:, head_size:].astype(jnp.bfloat16)
    keys, values = (
        lax.all_gather(own_keys, "shard", axis=0, tiled=True),
        lax.all_gather(own_values, "shard", axis=0, tiled=True),
    )

    def scores_of():
        raw_scores = jnp.einsum("thd,gd->htg", queries, keys, preferred_element_type=jnp.float32)
        return jnp.where(allowed[None], raw_scores, MASKED)

    scores = scores_of()
    row_max = jnp.max(scores, axis=-1, keepdims=True)
    log_total = row_max + jnp.log(jnp.sum(jnp.exp(scores - row_max), axis=-1, keepdims=True))
    probs_low = jnp.exp(scores - log_total).astype(jnp.bfloat16)
    attended = jnp.einsum("htg,gd->thd", probs_low, values, preferred_element_type=jnp.float32)
    attended = attended.reshape(row_count, heads_all).astype(jnp.bfloat16)
    middle = inputs + keep_mask * matmul(attended, out_full)
    inverse2 = lax.rsqrt(jnp.mean(middle * middle, axis=1, keepdims=True) + EPSILON)
    scaled2 = middle * inverse2
    normed_part = scaled2
    normed_part = (
        normed_part * lax.all_gather(mlp_gain, "shard", axis=0, tiled=True).astype(jnp.float32)
    ).astype(jnp.bfloat16)
    gate_pre = matmul(normed_part, lax.all_gather(w_gate, "shard", axis=0, tiled=True))
    up_pre = matmul(normed_part, lax.all_gather(w_up, "shard", axis=0, tiled=True))
    hidden = (jax.nn.gelu(gate_pre, approximate=True) * up_pre).astype(jnp.bfloat16)
    branch = matmul(hidden, lax.all_gather(w_down, "shard", axis=0, tiled=True))
    outputs = (middle + keep_mask * branch).astype(jnp.bfloat16)
    gain2, gate_full, up_full, down_full = (
        lax.all_gather(mlp_gain, "shard", axis=0, tiled=True),
        lax.all_gather(w_gate, "shard", axis=0, tiled=True),
        lax.all_gather(w_up, "shard", axis=0, tiled=True),
        lax.all_gather(w_down, "shard", axis=0, tiled=True),
    )
    normed2 = (scaled2 * gain2.astype(jnp.float32)).astype(jnp.bfloat16)
    grad_out = cotangent.astype(jnp.float32)
    grad_branch = (keep_mask * grad_out).astype(jnp.bfloat16)
    grad_down = lead_product(hidden, grad_branch)
    grad_hidden = trail_product(grad_branch, down_full)
    activated, gelu_pull = jax.vjp(
        lambda values_in: jax.nn.gelu(values_in, approximate=True), gate_pre
    )
    grad_gate = gelu_pull(grad_hidden * up_pre)[0].astype(jnp.bfloat16)
    grad_up = (grad_hidden * activated).astype(jnp.bfloat16)
    grad_gate_w = lead_product(normed2, grad_gate)
    grad_up_w = lead_product(normed2, grad_up)
    grad_normed2 = trail_product(grad_gate, gate_full) + trail_product(grad_up, up_full)
    grad_gain2 = jnp.sum(grad_normed2 * scaled2, axis=0)
    grad_middle = grad_out + norm_back(grad_normed2, scaled2, inverse2, gain2.astype(jnp.float32))
    mlp_grads = (
        lax.psum_scatter(
            grad_gain2.astype(jnp.bfloat16), "shard", scatter_dimension=0, tiled=True
        ).astype(jnp.float32),
        lax.psum_scatter(
            grad_gate_w.astype(jnp.bfloat16), "shard", scatter_dimension=0, tiled=True
        ).astype(jnp.float32),
        lax.psum_scatter(
            grad_up_w.astype(jnp.bfloat16), "shard", scatter_dimension=0, tiled=True
        ).astype(jnp.float32),
        lax.psum_scatter(
            grad_down.astype(jnp.bfloat16), "shard", scatter_dimension=0, tiled=True
        ).astype(jnp.float32),
    )
    gain1, query_full, keyval_full, out_full = (
        lax.all_gather(attn_gain, "shard", axis=0, tiled=True),
        lax.all_gather(w_query, "shard", axis=0, tiled=True),
        lax.all_gather(w_keyval, "shard", axis=0, tiled=True),
        lax.all_gather(w_out, "shard", axis=0, tiled=True),
    )
    grad_attn = (keep_mask * grad_middle).astype(jnp.bfloat16)
    grad_out_w = lead_product(attended, grad_attn)
    grad_attended = (
        trail_product(grad_attn, out_full)
        .astype(jnp.bfloat16)
        .reshape(row_count, head_count, head_size)
    )
    probs_full = jnp.exp(scores_of() - log_total)
    probs_again = probs_full.astype(jnp.bfloat16)
    grad_probs = jnp.einsum(
        "thd,gd->htg", grad_attended, values, preferred_element_type=jnp.float32
    )
    grad_values_all = jnp.einsum(
        "htg,thd->gd", probs_again, grad_attended, preferred_element_type=jnp.float32
    )
    row_delta = jnp.sum(probs_full * grad_probs, axis=-1, keepdims=True)
    grad_scores = (probs_full * (grad_probs - row_delta)).astype(jnp.bfloat16)
    grad_queries = jnp.einsum("htg,gd->thd", grad_scores, keys, preferred_element_type=jnp.float32)
    grad_keys_all = jnp.einsum(
        "htg,thd->gd", grad_scores, queries, preferred_element_type=jnp.float32
    )
    grad_own_keys, grad_own_values = (
        lax.psum_scatter(
            grad_keys_all.astype(jnp.bfloat16), "shard", scatter_dimension=0, tiled=True
        ).astype(jnp.float32),
        lax.psum_scatter(
            grad_values_all.astype(jnp.bfloat16), "shard", scatter_dimension=0, tiled=True
        ).astype(jnp.float32),
    )
    grad_query_proj = (
        (rotate(grad_queries, heads_cos, -heads_sin) * scaling)
        .reshape(row_count, heads_all)
        .astype(jnp.bfloat16)
    )
    grad_keyval_proj = jnp.concatenate(
        [rotate(grad_own_keys, cosine, -sine_part), grad_own_values], axis=1
    ).astype(jnp.bfloat16)
    grad_query_w = lead_product(normed1, grad_query_proj)
    grad_keyval_w = lead_product(normed1, grad_keyval_proj)
    grad_normed1 = trail_product(grad_query_proj, query_full) + trail_product(
        grad_keyval_proj, keyval_full
    )
    grad_gain1 = jnp.sum(grad_normed1 * scaled1, axis=0)
    grad_inputs = grad_middle + norm_back(
        grad_normed1, scaled1, inverse1, gain1.astype(jnp.float32)
    )
    attn_grads = (
        lax.psum_scatter(
            grad_gain1.astype(jnp.bfloat16), "shard", scatter_dimension=0, tiled=True
        ).astype(jnp.float32),
        lax.psum_scatter(
            grad_query_w.astype(jnp.bfloat16), "shard", scatter_dimension=0, tiled=True
        ).astype(jnp.float32),
        lax.psum_scatter(
            grad_keyval_w.astype(jnp.bfloat16), "shard", scatter_dimension=0, tiled=True
        ).astype(jnp.float32),
        lax.psum_scatter(
            grad_out_w.astype(jnp.bfloat16), "shard", scatter_dimension=0, tiled=True
        ).astype(jnp.float32),
    )
    summed_all = (
        lax.psum(attn_grads[0].astype(jnp.bfloat16), "rep").astype(jnp.float32),
        lax.psum(attn_grads[1].astype(jnp.bfloat16), "rep").astype(jnp.float32),
        lax.psum(attn_grads[2].astype(jnp.bfloat16), "rep").astype(jnp.float32),
        lax.psum(attn_grads[3].astype(jnp.bfloat16), "rep").astype(jnp.float32),
        lax.psum(mlp_grads[0].astype(jnp.bfloat16), "rep").astype(jnp.float32),
        lax.psum(mlp_grads[1].astype(jnp.bfloat16), "rep").astype(jnp.float32),
        lax.psum(mlp_grads[2].astype(jnp.bfloat16), "rep").astype(jnp.float32),
        lax.psum(mlp_grads[3].astype(jnp.bfloat16), "rep").astype(jnp.float32),
    )
    attn_grads = summed_all[:4]
    mlp_grads = summed_all[4:]
    return (
        outputs,
        grad_inputs,
        attn_grads[0],
        attn_grads[1],
        attn_grads[2],
        attn_grads[3],
        mlp_grads[0],
        mlp_grads[1],
        mlp_grads[2],
        mlp_grads[3],
    )


def solution(mesh):
    placed = (
        P(("rep", "shard"), None),
        P("rep", "shard"),
        P("shard"),
        P("shard", None),
        P("shard", None),
        P("shard", None),
        P("shard"),
        P("shard", None),
        P("shard", None),
        P("shard", None),
        P(("rep", "shard"), None),
    )
    return jax.shard_map(
        on_device,
        mesh=mesh,
        in_specs=placed,
        out_specs=(
            P(("rep", "shard"), None),
            P(("rep", "shard"), None),
            P("shard"),
            P("shard", None),
            P("shard", None),
            P("shard", None),
            P("shard"),
            P("shard", None),
            P("shard", None),
            P("shard", None),
        ),
        check_vma=False,
    )
```

profile of v0, /device:TPU:1, one launch (start us, length us, event | category | flops | bytes accessed | tf_op | source)
XLA Modules:
  0.0 1939.1 jit_solution(1622290492479480842)
XLA Ops:
  13.2 12.3 all-reduce
  26.9 16.1 all-reduce.8
  47.3 5.0 select_compare_fusion
  52.3 5.2 select_add_fusion
  57.9 2.7 all-gather.7.cloned.1.call-done
  60.7 1.7 fusion.81
  62.9 32.4 %all_gather.45 = bf16[1536,256]{1,0:T(8,128)(2,1)} all-gather(bf16[192,256]{1,0:T(8,128)(2,1)S(1)} %pad_maximum_fusion.1), channel_id=1, replica_groups=mesh['rep'=16,'shard'=8] {'shard'}, dimensions={0}, use_global_device_ids=true | all-gather | bytes 884736 | tf_op jit(solution)/shard_map/all_gather | solution.py:101
  95.3 31.5 %all_gather.44 = bf16[1536,256]{1,0:T(8,128)(2,1)S(1)} all-gather(bf16[192,256]{1,0:T(8,128)(2,1)S(1)} %slice.119), channel_id=1, replica_groups=mesh['rep'=16,'shard'=8] {'shard'}, dimensions={0}, use_global_device_ids=true | all-gather | bytes 884736 | tf_op jit(solution)/shard_map/all_gather | solution.py:102
  126.8 3.6 fusion.79
  132.1 2.4 fusion.10
  136.8 45.5 %all-gather.11.cloned.1.call-done = bf16[1024,1152]{1,0:T(8,128)(2,1)} async-done(((bf16[128,1152]{1,0:T(8,128)(2,1)}), bf16[1024,1152]{1,0:T(8,128)(2,1)}) %all-gather.11.cloned.1.call-update) | async-done | bytes 2359312 | tf_op jit(solution)/shard_map/all_gather | solution.py:86
  182.3 2.5 multiply_reduce_fusion.2
  185.0 176.9 %all-gather.15.cloned.1.call-done = bf16[1152,6912]{1,0:T(8,128)(2,1)} async-done(((bf16[144,6912]{1,0:T(8,128)(2,1)}), bf16[1152,6912]{1,0:T(8,128)(2,1)}) %all-gather.15.cloned.1.call-update) | async-done | bytes 15925264 | tf_op jit(solution)/shard_map/all_gather | solution.py:123
  361.9 11.9 fusion.88
  373.8 166.2 %all-gather.13.cloned.1.call-done = bf16[1152,6912]{1,0:T(8,128)(2,1)} async-done(((bf16[144,6912]{1,0:T(8,128)(2,1)}), bf16[1152,6912]{1,0:T(8,128)(2,1)}) %all-gather.13.cloned.1.call-update) | async-done | bytes 15925264 | tf_op jit(solution)/shard_map/all_gather | solution.py:122
  539.9 11.9 fusion.87
  551.8 166.2 %all-gather.17.cloned.1.call-done = bf16[6912,1152]{1,0:T(8,128)(2,1)} async-done(((bf16[864,1152]{1,0:T(8,128)(2,1)}), bf16[6912,1152]{1,0:T(8,128)(2,1)}) %all-gather.17.cloned.1.call-update) | async-done | bytes 15925264 | tf_op jit(solution)/shard_map/all_gather | solution.py:125
  718.0 13.9 multiply_convert_fusion
  731.9 11.6 fusion.89
  743.5 13.1 multiply_reduce_fusion
  758.3 2.8 convolution_convert_fusion.6
  761.1 4.1 fusion.7
  765.3 1.8 fusion.9
  770.3 4.7 fusion.15
  775.1 63.6 %reduce-scatter.9.cloned.1.call-done = bf16[192,256]{1,0:T(8,128)(2,1)} async-done(((bf16[1536,256]{1,0:T(8,128)(2,1)}), bf16[192,256]{1,0:T(8,128)(2,1)}) %reduce-scatter.9.cloned.1.call-update) | async-done | bytes 98320 | tf_op jit(solution)/shard_map/reduce_scatter | solution.py:190
  840.7 72.7 %reduce-scatter.11.cloned.1.call-done = bf16[192,256]{1,0:T(8,128)(2,1)} async-done(((bf16[1536,256]{1,0:T(8,128)(2,1)}), bf16[192,256]{1,0:T(8,128)(2,1)}) %reduce-scatter.11.cloned.1.call-update) | async-done | bytes 98320 | tf_op jit(solution)/shard_map/reduce_scatter | solution.py:193
  913.3 2.5 convolution_convert_fusion.5
  915.9 2.4 convolution_convert_fusion.3
  918.4 2.7 convolution_bitcast_fusion.2
  922.3 2.3 convolution_convert_fusion.4
  924.7 10.7 convolution_convert_fusion.2
  935.5 9.8 convolution_convert_fusion
  945.4 9.7 convolution_convert_fusion.1
  955.3 34.3 %reduce-scatter.15.cloned.1.call-done = bf16[144,512]{1,0:T(8,128)(2,1)} async-done(((bf16[1152,512]{1,0:T(8,128)(2,1)}), bf16[144,512]{1,0:T(8,128)(2,1)}) %reduce-scatter.15.cloned.1.call-update) | async-done | bytes 147472 | tf_op jit(solution)/shard_map/reduce_scatter | solution.py:221
  989.5 80.9 %reduce-scatter.17.cloned.1.call-done = bf16[128,1152]{1,0:T(8,128)(2,1)} async-done(((bf16[1024,1152]{1,0:T(8,128)(2,1)}), bf16[128,1152]{1,0:T(8,128)(2,1)}) %reduce-scatter.17.cloned.1.call-update) | async-done | bytes 294928 | tf_op jit(solution)/shard_map/reduce_scatter | solution.py:224
  1070.4 79.6 %reduce-scatter.13.cloned.1.call-done = bf16[144,1024]{1,0:T(8,128)(2,1)} async-done(((bf16[1152,1024]{1,0:T(8,128)(2,1)}), bf16[144,1024]{1,0:T(8,128)(2,1)}) %reduce-scatter.13.cloned.1.call-update) | async-done | bytes 294928 | tf_op jit(solution)/shard_map/reduce_scatter | solution.py:218
  1150.0 195.5 %reduce-scatter.23.cloned.1.call-done = bf16[864,1152]{1,0:T(8,128)(2,1)} async-done(((bf16[6912,1152]{1,0:T(8,128)(2,1)}), bf16[864,1152]{1,0:T(8,128)(2,1)}) %reduce-scatter.23.cloned.1.call-update) | async-done | bytes 1990672 | tf_op jit(solution)/shard_map/reduce_scatter | solution.py:158
  1345.5 199.4 %reduce-scatter.21.cloned.1.call-done = bf16[144,6912]{1,0:T(8,128)(2,1)} async-done(((bf16[1152,6912]{1,0:T(8,128)(2,1)}), bf16[144,6912]{1,0:T(8,128)(2,1)}) %reduce-scatter.21.cloned.1.call-update) | async-done | bytes 1990672 | tf_op jit(solution)/shard_map/reduce_scatter | solution.py:155
  1544.9 200.1 %reduce-scatter.19.cloned.1.call-done = bf16[144,6912]{1,0:T(8,128)(2,1)} async-done(((bf16[1152,6912]{1,0:T(8,128)(2,1)}), bf16[144,6912]{1,0:T(8,128)(2,1)}) %reduce-scatter.19.cloned.1.call-update) | async-done | bytes 1990672 | tf_op jit(solution)/shard_map/reduce_scatter | solution.py:152
  1745.7 10.9 fusion.16
  1758.2 21.2 %all-reduce.7 = (bf16[1152]{0:T(1024)(128)(2,1)S(1)}, bf16[1152]{0:T(1024)(128)(2,1)S(1)}) all-reduce(bf16[1152]{0:T(1024)(128)(2,1)S(1)} %get-tuple-element.33, bf16[1152]{0:T(1024)(128)(2,1)S(1)} %copy-done.27), channel_id=4, replica_groups=mesh['rep'=16,'shard'=8] {'shard'}, use_global_device_ids=true, to_apply=%region_13.15.clone | all-reduce | flops 2304 | bytes 9216
  1779.5 32.6 %all-reduce.5 = (bf16[144]{0:T(256)(128)(2,1)S(1)}, bf16[144]{0:T(256)(128)(2,1)S(1)}) all-reduce(bf16[144]{0:T(256)(128)(2,1)S(1)} %dynamic-slice.13, bf16[144]{0:T(256)(128)(2,1)S(1)} %dynamic-slice.15), channel_id=1, replica_groups=mesh['rep'=16,'shard'=8] {'rep'}, use_global_device_ids=true, to_apply=%region_14.16 | all-reduce | flops 288 | bytes 1152 | tf_op jit(solution)/shard_map/psum | solution.py:229
  1814.4 104.2 %all-reduce.11.cloned.1.call-done = (bf16[144,1024]{1,0:T(8,128)(2,1)}, bf16[144,512]{1,0:T(8,128)(2,1)}, bf16[128,1152]{1,0:T(8,128)(2,1)}, bf16[144,6912]{1,0:...) async-done(((bf16[144,1024]{1,0:T(8,128)(2,1)}, bf16[144,512]{1,0:T(8,128)(2,1)}, bf16[128,1152]{1,0:T(8,128)(2,1)}, bf16[144,6912]{1,0:T(8,128)(2,1)}, ...) | async-done | bytes 6709264 | tf_op jit(solution)/shard_map/psum | solution.py:230
  1918.7 2.0 convert_element_type.188
  1922.3 1.8 convert_element_type.192
  1924.1 3.9 convert_element_type.196
  1928.0 2.2 convert_element_type.198
  1930.2 2.2 convert_element_type.200
  (149 shorter events, 29.5 us)
Async XLA Ops:
  7.2 4.8 copy-start.28
  7.2 40.0 %copy-start.20 = (pred[1536]{0:T(1024)(128)(4,1)S(1)}, pred[1536]{0:T(1024)(128)(4,1)}, u32[]{:S(2)}) copy-start(pred[1536]{0:T(1024)(128)(4,1)} %constant.199) | copy-start | bytes 4612
  7.2 40.0 %copy-start.21 = (pred[1536]{0:T(1024)(128)(4,1)S(1)}, pred[1536]{0:T(1024)(128)(4,1)}, u32[]{:S(2)}) copy-start(pred[1536]{0:T(1024)(128)(4,1)} %constant.198) | copy-start | bytes 4612
  7.2 40.0 %copy-start.22 = (pred[1536]{0:T(1024)(128)(4,1)S(1)}, pred[1536]{0:T(1024)(128)(4,1)}, u32[]{:S(2)}) copy-start(pred[1536]{0:T(1024)(128)(4,1)} %constant.197) | copy-start | bytes 4612
  7.2 40.0 %copy-start.23 = (pred[1536]{0:T(1024)(128)(4,1)S(1)}, pred[1536]{0:T(1024)(128)(4,1)}, u32[]{:S(2)}) copy-start(pred[1536]{0:T(1024)(128)(4,1)} %constant.196) | copy-start | bytes 4612
  7.2 40.0 %copy-start.24 = (pred[1536]{0:T(1024)(128)(4,1)S(1)}, pred[1536]{0:T(1024)(128)(4,1)}, u32[]{:S(2)}) copy-start(pred[1536]{0:T(1024)(128)(4,1)} %constant.195) | copy-start | bytes 4612
  7.3 40.0 %copy-start.25 = (pred[1536]{0:T(1024)(128)(4,1)S(1)}, pred[1536]{0:T(1024)(128)(4,1)}, u32[]{:S(2)}) copy-start(pred[1536]{0:T(1024)(128)(4,1)} %constant.194) | copy-start | bytes 4612
  7.3 40.0 %copy-start.26 = (pred[1536]{0:T(1024)(128)(4,1)S(1)}, pred[1536]{0:T(1024)(128)(4,1)}, u32[]{:S(2)}) copy-start(pred[1536]{0:T(1024)(128)(4,1)} %constant.193) | copy-start | bytes 4612
  7.3 19.1 copy-start.29
  7.3 19.3 copy-start.30
  7.3 39.7 %copy-start.1 = (bf16[192,1152]{1,0:T(8,128)(2,1)S(1)}, bf16[192,1152]{1,0:T(8,128)(2,1)}, u32[]{:S(2)}) copy-start(bf16[192,1152]{1,0:T(8,128)(2,1)} %param.17) | copy-start | bytes 1327108
  7.3 53.4 %all-gather.7.cloned.1.call-start = ((), (), s32[]{:S(2)}) async-start(), calls=%async_computation.8 | async-start | bytes 1327104 | tf_op jit(solution)/shard_map/all_gather | solution.py:85
  8.0 118.8 %all-gather.9.cloned.1.call-start = ((), (), s32[]{:S(2)}) async-start(), calls=%async_computation.9 | async-start | bytes 2654208 | tf_op jit(solution)/shard_map/all_gather | solution.py:84
  8.8 173.5 %all-gather.11.cloned.1.call-start = ((), (), s32[]{:S(2)}) async-start(), calls=%async_computation.10 | async-start | bytes 2654208 | tf_op jit(solution)/shard_map/all_gather | solution.py:86
  9.5 352.4 %all-gather.15.cloned.1.call-start = ((), (), s32[]{:S(2)}) async-start(), calls=%async_computation.12 | async-start | bytes 17915904 | tf_op jit(solution)/shard_map/all_gather | solution.py:123
  10.1 529.8 %all-gather.13.cloned.1.call-start = ((), (), s32[]{:S(2)}) async-start(), calls=%async_computation.11 | async-start | bytes 17915904 | tf_op jit(solution)/shard_map/all_gather | solution.py:122
  10.7 707.3 %all-gather.17.cloned.1.call-start = ((), (), s32[]{:S(2)}) async-start(), calls=%async_computation.13 | async-start | bytes 17915904 | tf_op jit(solution)/shard_map/all_gather | solution.py:125
  11.3 827.4 %reduce-scatter.9.cloned.1.call-start = ((), (), s32[]{:S(2)}) async-start(), calls=%async_computation.14 | async-start | bytes 884736 | tf_op jit(solution)/shard_map/reduce_scatter | solution.py:190
  62.9 69.2 %copy-start.12 = (f32[192,128]{1,0:T(8,128)}, f32[192,128]{1,0:T(8,128)S(1)}, u32[]{:S(2)}) copy-start(f32[192,128]{1,0:T(8,128)S(1)} %get-tuple-element.63) | copy-start | bytes 294916
  126.8 8.9 copy-start.3
  132.1 2.4 copy-start.13
  132.1 2.4 copy-start.15
  134.6 2.2 copy-start
  373.8 344.2 %copy-start.8 = (bf16[192,1152]{1,0:T(8,128)(2,1)S(1)}, bf16[192,1152]{1,0:T(8,128)(2,1)}, u32[]{:S(2)}) copy-start(bf16[192,1152]{1,0:T(8,128)(2,1)} %param.27) | copy-start | bytes 1327108
  756.6 4.4 copy-start.4
  758.3 7.0 slice-start
  761.0 4.2 copy-start.10
  761.1 4.2 slice-start.1
  765.3 3.2 copy-start.14
  765.3 3.2 copy-start.16
  767.1 1.4 copy-start.5
  770.2 143.1 %reduce-scatter.11.cloned.1.call-start = ((), (), s32[]{:S(2)}) async-start(), calls=%async_computation.15 | async-start | bytes 884736 | tf_op jit(solution)/shard_map/reduce_scatter | solution.py:193
  775.0 214.5 %reduce-scatter.15.cloned.1.call-start = ((), (), s32[]{:S(2)}) async-start(), calls=%async_computation.17 | async-start | bytes 1327104 | tf_op jit(solution)/shard_map/reduce_scatter | solution.py:221
  840.7 77.7 %copy-start.17 = (bf16[192,128]{1,0:T(8,128)(2,1)}, bf16[192,128]{1,0:T(8,128)(2,1)S(1)}, u32[]{:S(2)}) copy-start(bf16[192,128]{1,0:T(8,128)(2,1)S(1)} %get-tuple-element.61) | copy-start | bytes 147460
  915.9 154.5 %reduce-scatter.17.cloned.1.call-start = ((), (), s32[]{:S(2)}) async-start(), calls=%async_computation.18 | async-start | bytes 2654208 | tf_op jit(solution)/shard_map/reduce_scatter | solution.py:224
  918.4 231.7 %reduce-scatter.13.cloned.1.call-start = ((), (), s32[]{:S(2)}) async-start(), calls=%async_computation.16 | async-start | bytes 2654208 | tf_op jit(solution)/shard_map/reduce_scatter | solution.py:218
  921.1 3.6 copy-start.9
  924.7 420.9 %reduce-scatter.23.cloned.1.call-start = ((), (), s32[]{:S(2)}) async-start(), calls=%async_computation.21 | async-start | bytes 17915904 | tf_op jit(solution)/shard_map/reduce_scatter | solution.py:158
  935.5 609.4 %reduce-scatter.21.cloned.1.call-start = ((), (), s32[]{:S(2)}) async-start(), calls=%async_computation.20 | async-start | bytes 17915904 | tf_op jit(solution)/shard_map/reduce_scatter | solution.py:155
  945.3 799.6 %reduce-scatter.19.cloned.1.call-start = ((), (), s32[]{:S(2)}) async-start(), calls=%async_computation.19 | async-start | bytes 17915904 | tf_op jit(solution)/shard_map/reduce_scatter | solution.py:152
  955.1 963.6 %all-reduce.11.cloned.1.call-start = ((), (), s32[]{:S(2)}) async-start(), calls=%async_computation.22 | async-start | bytes 13418496 | tf_op jit(solution)/shard_map/psum | solution.py:230
  1745.6 10.9 copy-start.2
  1745.6 11.8 copy-start.11
  1745.6 11.8 copy-start.18
  1745.6 11.8 copy-start.19
  1756.5 1.7 copy-start.27
  1918.7 9.3 copy-start.7
  1924.1 6.1 copy-start.6
Sparse Core Ops, SparseCore 0:
  10.5 50.1 all-gather.6
  63.0 62.7 all-gather.8
  128.1 54.1 all-gather.10
  184.5 177.3 all-gather.14
  364.0 175.8 all-gather.12
  542.1 175.8 all-gather.16
  770.4 68.2 reduce-scatter.8
  842.3 71.0 reduce-scatter.10
  917.1 72.4 reduce-scatter.14
  993.7 76.7 reduce-scatter.16
  1074.2 75.7 reduce-scatter.12
  1154.4 191.0 reduce-scatter.22
  1350.0 194.7 reduce-scatter.20
  1549.2 195.6 reduce-scatter.18
  1748.1 170.5 all-reduce.10
where the time goes:
time: 1940 us
  waiting for transfers between devices  1590 us (82%)
  blocking collectives  146 us (8%)
  matrix products  139 us (7%)
  other arithmetic  38 us (2%)
    reduce_scatter x1, waiting for transfers between devices, on_device(): lax.psum_scatter(grad_gate_w.astype(jnp.bfloat16), 'shard', scatter_dimen...  200 us
    reduce_scatter x1, waiting for transfers between devices, on_device(): lax.psum_scatter(grad_up_w.astype(jnp.bfloat16), 'shard', scatter_dimensi...  199 us
    reduce_scatter x1, waiting for transfers between devices, on_device(): lax.psum_scatter(grad_down.astype(jnp.bfloat16), 'shard', scatter_dimensi...  195 us
    all_gather x1, waiting for transfers between devices, on_device(): lax.all_gather(w_up, 'shard', axis=0, tiled=True)  177 us
    all_gather x1, waiting for transfers between devices, on_device(): branch = matmul(hidden, lax.all_gather(w_down, 'shard', axis=0, tiled=True))  166 us
    all_gather x1, waiting for transfers between devices, on_device(): lax.all_gather(w_gate, 'shard', axis=0, tiled=True)  166 us
    psum x1, waiting for transfers between devices, on_device(): lax.psum(attn_grads[1].astype(jnp.bfloat16), 'rep').astype(jnp.float32)  104 us
    reduce_scatter x1, waiting for transfers between devices, on_device(): lax.psum_scatter(grad_out_w.astype(jnp.bfloat16), 'shard', scatter_dimens...  80.9 us
  transfers between devices with their start and end apart: 15, of which 14 were waited for; matrix products, arithmetic and copies ran while one was open for 6% of the time, Pallas kernels for 0%

commit v1 on v0

v1 whole, which is shorter than its diff:
```python
import functools

import jax
import jax.numpy as jnp
from jax import lax
from jax.experimental import pallas as pl
from jax.experimental.pallas import tpu as pltpu
from jax.sharding import PartitionSpec as P

MESH = pl.DeviceIdType.MESH
WINDOW = 512
EPSILON = 1e-06
MASKED = -1e30
VMEM_LIMIT = 60 * 2**20
FF_DEV = 864
FF_PAD = 896
PAIRS = FF_PAD // 128
BEHIND = 4


def matmul(former, latter):
    return jnp.dot(former, latter, preferred_element_type=jnp.float32)


def lead_product(former, latter):
    return lax.dot_general(
        former, latter, (((0,), (0,)), ((), ())), preferred_element_type=jnp.float32
    )


def trail_product(former, latter):
    return lax.dot_general(
        former, latter, (((1,), (1,)), ((), ())), preferred_element_type=jnp.float32
    )


class Place:
    def __init__(self):
        rep, shard = lax.axis_index("rep"), lax.axis_index("shard")
        self.rep, self.shard = rep, shard
        self.y, self.z_lo, self.core = rep // 4, (rep // 2) % 2, rep % 2
        self.z_hi, self.x = shard // 4, shard % 4

    def device(self, dx=0, dy=0, mirror=0, swap_lo=0, sibling=0):
        z_lo = (self.z_lo + mirror + swap_lo) % 2
        rep = (((self.y + dy) % 4) * 2 + z_lo) * 2 + (self.core + sibling) % 2
        return (rep, ((self.z_hi + mirror) % 2) * 4 + (self.x + dx) % 4)

    def shard_at(self, j, p):
        return ((self.z_hi + p) % 2) * 4 + (self.x + STEPS[j]) % 4


STEPS = (0, 1, 3, 2)


class Wire:
    def __init__(self, send_sems, recv_sems):
        self.send_sems, self.recv_sems, self.made = send_sems, recv_sems, []

    def copy(self, src, dst, device):
        k = len(self.made)
        made = pltpu.make_async_remote_copy(
            src_ref=src,
            dst_ref=dst,
            send_sem=self.send_sems.at[k],
            recv_sem=self.recv_sems.at[k],
            device_id=device,
            device_id_type=MESH,
        )
        self.made.append(made)
        return made

    def drain(self):
        for made in self.made:
            made.wait_send()


def greet(devices):
    barrier = pltpu.get_barrier_semaphore()
    for device in devices:
        pl.semaphore_signal(barrier, inc=1, device_id=device, device_id_type=MESH)
    pl.semaphore_wait(barrier, len(devices))


GATHER_HOPS = (
    ((0, 0), (0, 1), 0, 0, 1),
    ((0, 0), (2, 0), 0, 1, 0),
    ((0, 0), (1, 0), 0, 3, 0),
    ((0, 1), (2, 1), 0, 1, 0),
    ((0, 1), (1, 1), 0, 3, 0),
    ((2, 0), (3, 0), 1, 1, 0),
    ((1, 0), (3, 0), 2, 3, 0),
    ((2, 1), (3, 1), 1, 1, 0),
    ((1, 1), (3, 1), 2, 3, 0),
)


def gather_tree(wire, place, own, slot, cut, absolute):
    copies = []
    for source, target, part, dx, mirror in GATHER_HOPS:
        src = own if source == (0, 0) else slot(*source)
        dst = slot(*(source if absolute else target))
        copies.append(wire.copy(cut(src, part), cut(dst, part), place.device(dx=dx, mirror=mirror)))
    return copies


def spread_kernel(
    misc, qkv, wo, gu, gb, o_misc, o_qkv, o_wo, o_gu, o_gb, local_sems, send_sems, recv_sems
):
    place = Place()
    wire = Wire(send_sems, recv_sems)
    core = place.core
    others = [(j, p) for p in (0, 1) for j in range(4) if (j, p) != (0, 0)]
    group = [place.device(dx=STEPS[j], mirror=p) for j, p in others]
    sequence = [(place.rep, place.shard_at(j, p)) for j, p in others]
    sibling = place.device(sibling=1)
    me = place.shard
    greet([sibling] + group + [d for d, (j, p) in zip(sequence, others) if p == 1])

    def cut_qkv(ref, part):
        start, size = ((0, 768), (0, 384), (384, 384))[part]
        return ref.at[:, pl.ds(pl.multiple_of(core * 768 + start, 128), size)]

    def cut_wo(ref, part):
        start, size = ((0, 64), (0, 32), (32, 32))[part]
        return ref.at[pl.ds(pl.multiple_of(core * 64 + start, 32), size)]

    def cut_gb(ref, part):
        return ref if part == 0 else ref.at[pl.ds((part - 1) * 96, 96)]

    def cut_gu(ref):
        return ref.at[:, pl.ds(pl.multiple_of(core * FF_PAD, 128), FF_PAD)]

    locals_ = []
    for k, (src, dst) in enumerate(
        [
            (misc, o_misc.at[me]),
            (qkv, o_qkv.at[me]),
            (wo, o_wo.at[me]),
            (gu.at[me], o_gu.at[me]),
            (gb, o_gb.at[0, 0]),
        ]
    ):
        copy = pltpu.make_async_copy(src, dst, local_sems.at[k])
        copy.start()
        locals_.append(copy)

    slot_qkv = lambda j, p: o_qkv.at[place.shard_at(j, p)]
    slot_wo = lambda j, p: o_wo.at[place.shard_at(j, p)]
    slot_gb = lambda j, p: o_gb.at[j, p]
    misc_copies = [wire.copy(misc, o_misc.at[me], device) for device in sequence]
    trees = [
        gather_tree(wire, place, qkv, slot_qkv, cut_qkv, True),
        gather_tree(wire, place, wo, slot_wo, cut_wo, True),
        gather_tree(wire, place, gb, slot_gb, cut_gb, False),
    ]
    gu_copies = [
        wire.copy(cut_gu(gu.at[place.shard_at(j, p)]), cut_gu(o_gu.at[me]), device)
        for (j, p), device in zip(others, group)
    ]
    passed = {}
    for j, p in others:
        at = place.shard_at(j, p)
        passed[j, p] = [
            wire.copy(cut_qkv(o_qkv.at[at], 0), cut_qkv(o_qkv.at[at], 0), sibling),
            wire.copy(cut_wo(o_wo.at[at], 0), cut_wo(o_wo.at[at], 0), sibling),
        ]
    gu_passed = []
    for j, p in others:
        at = place.shard_at((0, 2, 1, 3)[j], p)
        gu_passed.append(wire.copy(cut_gu(o_gu.at[at]), cut_gu(o_gu.at[at]), sibling))

    for copy in misc_copies:
        copy.start()
    for tree in trees[:2]:
        for k in (0, 1, 2):
            tree[k].start()

    def then(k, nexts, slots):
        for tree in trees[:2]:
            tree[k].wait_recv()
            for n in nexts:
                tree[n].start()
        for s in slots:
            for copy in passed[s]:
                copy.start()

    then(0, (3, 4), [(0, 1)])
    then(1, (5,), [(2, 0)])
    then(2, (6,), [(1, 0)])
    then(3, (7,), [(2, 1)])
    then(4, (8,), [(1, 1)])
    for k in (0, 1, 2):
        trees[2][k].start()
    for copy in gu_copies:
        copy.start()
    then(5, (), [])
    then(6, (), [(3, 0)])
    then(7, (), [])
    then(8, (), [(3, 1)])
    gb_tree = trees[2]
    for k, nexts in ((0, (3, 4)), (1, (5,)), (2, (6,)), (3, (7,)), (4, (8,))):
        gb_tree[k].wait_recv()
        for n in nexts:
            gb_tree[n].start()
    for copy, onward in zip(gu_copies, gu_passed):
        copy.wait_recv()
        onward.start()
    for k in (5, 6, 7, 8):
        gb_tree[k].wait_recv()
    for copy in misc_copies + gu_passed + [c for cs in passed.values() for c in cs]:
        copy.wait_recv()
    for copy in locals_:
        copy.wait()
    wire.drain()


ANY = pl.BlockSpec(memory_space=pl.ANY)


def comm_params(collective_id):
    return pltpu.CompilerParams(
        collective_id=collective_id, has_side_effects=True, vmem_limit_bytes=VMEM_LIMIT
    )


def spread(misc, qkv, wo, gu, gb):
    shape = lambda *s: jax.ShapeDtypeStruct(s, jnp.bfloat16)
    return pl.pallas_call(
        spread_kernel,
        out_shape=(
            shape(8, *misc.shape),
            shape(8, *qkv.shape),
            shape(8, *wo.shape),
            shape(*gu.shape),
            shape(4, 2, *gb.shape),
        ),
        in_specs=[ANY] * 5,
        out_specs=(ANY,) * 5,
        scratch_shapes=[
            pltpu.SemaphoreType.DMA((5,)),
            pltpu.SemaphoreType.DMA((64,)),
            pltpu.SemaphoreType.DMA((64,)),
        ],
        compiler_params=comm_params(1),
        name="spread_weights",
    )(misc, qkv, wo, gu, gb)


def window_kernel(reverse, own, out, send_sems, recv_sems):
    rep, shard = lax.axis_index("rep"), lax.axis_index("shard")
    barrier = pltpu.get_barrier_semaphore()
    sign = -1 if reverse else 1

    def inside(i):
        return jnp.logical_and(shard + i >= 0, shard + i < 8)

    for i in range(1, BEHIND + 1):

        @pl.when(inside(-sign * i))
        def _():
            pl.semaphore_signal(
                barrier, inc=1, device_id=(rep, shard - sign * i), device_id_type=MESH
            )

    targets = jnp.minimum(shard if reverse else 7 - shard, BEHIND)

    @pl.when(targets > 0)
    def _():
        pl.semaphore_wait(barrier, targets)

    copies = []
    for i in range(1, BEHIND + 1):
        copy = pltpu.make_async_remote_copy(
            src_ref=own.at[i] if reverse else own,
            dst_ref=out.at[i - 1],
            send_sem=send_sems.at[i],
            recv_sem=recv_sems.at[i],
            device_id=(rep, shard + sign * i),
            device_id_type=MESH,
        )
        copies.append(copy)
        pl.when(inside(sign * i))(copy.start)
    for i, copy in enumerate(copies):
        pl.when(inside(-sign * (i + 1)))(copy.wait_recv)
        pl.when(inside(sign * (i + 1)))(copy.wait_send)


def window(own, reverse, collective_id, name):
    block = own.shape[-2:]
    return pl.pallas_call(
        functools.partial(window_kernel, reverse),
        out_shape=jax.ShapeDtypeStruct((BEHIND, *block), jnp.bfloat16),
        in_specs=[ANY],
        out_specs=ANY,
        scratch_shapes=[
            pltpu.SemaphoreType.DMA((BEHIND + 1,)),
            pltpu.SemaphoreType.DMA((BEHIND + 1,)),
        ],
        compiler_params=comm_params(collective_id),
        name=name,
    )(own)


class SumTree:
    def __init__(self, wire, place, slot, cut, half_a, half_b, from_m, from_p, from_z):
        self.slot, self.cut = slot, cut
        self.half_a, self.half_b, self.from_m, self.from_p = half_a, half_b, from_m, from_p
        self.from_z = from_z
        plus, minus = place.device(dx=1), place.device(dx=3)
        self.far, self.near = {}, {}
        for p in (0, 1):
            self.far[p] = (
                wire.copy(cut(slot(3, p), 1), half_a.at[p], plus),
                wire.copy(cut(slot(3, p), 2), half_b.at[p], minus),
            )
            self.near[p] = (
                wire.copy(slot(1, p), from_m.at[p], plus),
                wire.copy(slot(2, p), from_p.at[p], minus),
            )
        self.last = wire.copy(slot(0, 1), from_z, place.device(mirror=1))

    def send_far(self):
        for p in (0, 1):
            for copy in self.far[p]:
                copy.start()

    def send_near(self):
        for p in (0, 1):
            for copy, part, half, j in (
                (self.far[p][0], 1, self.half_a, 1),
                (self.far[p][1], 2, self.half_b, 2),
            ):
                copy.wait_recv()
                add_into(self.cut(self.slot(j, p), part), half.at[p])
                self.near[p][j - 1].start()

    def send_last(self):
        for p in (1, 0):
            for copy, source in zip(self.near[p], (self.from_m, self.from_p)):
                copy.wait_recv()
                add_into(self.slot(0, p), source.at[p])
            if p == 1:
                self.last.start()

    def finish(self):
        self.last.wait_recv()
        return self.slot(0, 0)[...].astype(jnp.float32) + self.from_z[...].astype(jnp.float32)


def add_into(target, source):
    target[...] = (target[...].astype(jnp.float32) + source[...].astype(jnp.float32)).astype(
        target.dtype
    )


ROOT = 0.7978845608028654
CUBE = 0.044715


def ff_kernel(
    own_n, gb_all, wgu_all, wd_all,
    o_gn, o_br, o_dgu, o_dd,
    nbuf, gb, wgu, wd, gh, hid, ggu, part_g, part_b, out_f32, dgu_tile,
    g_ha, g_hb, g_fm, g_fp, g_fz, b_ha, b_hb, b_fm, b_fp, b_fz,
    local_sems, send_sems, recv_sems,
):
    place = Place()
    wire = Wire(send_sems, recv_sems)
    loads = [
        pltpu.make_async_copy(src, dst, local_sems.at[k])
        for k, (src, dst) in enumerate(
            [(own_n, nbuf.at[0, 0]), (wd_all, wd), (gb_all, gb), (wgu_all, wgu)]
        )
    ]
    for load in loads:
        load.start()
    greet([place.device(dx=1), place.device(dx=3), place.device(mirror=1)])

    def cut(ref, part):
        return ref if part == 0 else ref.at[pl.ds((part - 1) * 96, 96)]

    slot_n = lambda j, p: nbuf.at[j, p]
    tree = gather_tree(wire, place, nbuf.at[0, 0], slot_n, cut, False)
    sum_g = SumTree(
        wire, place, lambda j, p: part_g.at[j, p], cut, g_ha, g_hb, g_fm, g_fp, g_fz
    )
    sum_b = SumTree(
        wire, place, lambda j, p: part_b.at[j, p], cut, b_ha, b_hb, b_fm, b_fp, b_fz
    )
    loads[0].wait()
    for k in (0, 1, 2):
        tree[k].start()
    loads[1].wait()
    loads[2].wait()

    def back_hidden(j):
        rows = jnp.concatenate([gb[j, 0], gb[j, 1]], axis=0)
        gh[j] = trail_product(rows, wd[...])

    def onward(k, nexts):
        tree[k].wait_recv()
        for n in nexts:
            tree[n].start()

    def forward(j):
        rows = jnp.concatenate([nbuf[j, 0], nbuf[j, 1]], axis=0)

        def tile(t, carry):
            columns = pl.ds(pl.multiple_of(t * 256, 256), 256)
            narrow = pl.ds(pl.multiple_of(t * 128, 128), 128)
            both = matmul(rows, wgu[:, columns])
            gate, up = both[:, :128], both[:, 128:]
            square = gate * gate
            curve = jnp.tanh(ROOT * gate * (1.0 + CUBE * square))
            half_up = 0.5 * (1.0 + curve)
            active = gate * half_up
            slope = half_up + 0.5 * gate * (1.0 - curve * curve) * (
                ROOT * (1.0 + 3.0 * CUBE * square)
            )
            back = gh[j, :, narrow]
            hid[j, :, narrow] = (active * up).astype(jnp.bfloat16)
            ggu[j, :, columns] = jnp.concatenate(
                [(back * up * slope).astype(jnp.bfloat16), (back * active).astype(jnp.bfloat16)],
                axis=1,
            )
            return carry

        lax.fori_loop(0, PAIRS, tile, 0)

    def back_normed(j):
        for start, size in ((0, 512), (512, 512), (1024, 128)):
            block = trail_product(ggu[j], wgu[start : start + size, :]).astype(jnp.bfloat16)
            part_g[j, 0, :, start : start + size] = block[:192]
            part_g[j, 1, :, start : start + size] = block[192:]

    def down(j):
        for start, size in ((0, 512), (512, 512), (1024, 128)):
            block = matmul(hid[j], wd[:, start : start + size]).astype(jnp.bfloat16)
            part_b[j, 0, :, start : start + size] = block[:192]
            part_b[j, 1, :, start : start + size] = block[192:]

    for j in range(4):
        back_hidden(j)
    onward(0, (3, 4))
    onward(1, (5,))
    onward(2, (6,))
    loads[3].wait()
    forward(0)
    onward(3, (7,))
    onward(4, (8,))
    forward(1)
    forward(2)
    for k in (5, 6, 7, 8):
        onward(k, ())
    forward(3)
    back_normed(3)
    sum_g.send_far()
    back_normed(1)
    back_normed(2)
    sum_g.send_near()
    down(3)
    sum_b.send_far()
    back_normed(0)
    down(1)
    down(2)
    sum_g.send_last()
    sum_b.send_near()
    down(0)

    hid_rows = hid.reshape(4 * 384, FF_PAD)
    ggu_rows = ggu.reshape(4 * 384, 2 * FF_PAD)
    n_rows = nbuf.reshape(4 * 384, 1152)
    gb_rows = gb.reshape(4 * 384, 1152)

    def grad_gu(t, carry):
        columns = pl.ds(pl.multiple_of(t * 256, 256), 256)
        dgu_tile[:, columns] = lead_product(n_rows[...], ggu_rows[:, columns]).astype(jnp.bfloat16)
        return carry

    lax.fori_loop(0, PAIRS, grad_gu, 0)
    store_gu = pltpu.make_async_copy(dgu_tile, o_dgu, local_sems.at[4])
    store_gu.start()

    part_dd = lead_product(hid_rows[...], gb_rows[...])
    wd[...] = part_dd.astype(jnp.bfloat16)
    store_d = pltpu.make_async_copy(wd, o_dd, local_sems.at[5])
    store_d.start()
    sum_b.send_last()
    out_f32[0] = sum_g.finish()
    out_f32[1] = sum_b.finish()
    stores = [
        store_gu,
        store_d,
        pltpu.make_async_copy(out_f32.at[0], o_gn, local_sems.at[6]),
        pltpu.make_async_copy(out_f32.at[1], o_br, local_sems.at[7]),
    ]
    for store in stores[2:]:
        store.start()
    for store in stores:
        store.wait()
    wire.drain()


def feed_forward(own_n, gb_all, wgu_all, wd_all):
    bf, f32 = jnp.bfloat16, jnp.float32
    vm = pltpu.VMEM
    tokens, width = own_n.shape
    sums = [
        vm((2, 96, width), bf),
        vm((2, 96, width), bf),
        vm((2, tokens, width), bf),
        vm((2, tokens, width), bf),
        vm((tokens, width), bf),
    ]
    return pl.pallas_call(
        ff_kernel,
        out_shape=(
            jax.ShapeDtypeStruct((tokens, width), f32),
            jax.ShapeDtypeStruct((tokens, width), f32),
            jax.ShapeDtypeStruct(wgu_all.shape, bf),
            jax.ShapeDtypeStruct(wd_all.shape, bf),
        ),
        in_specs=[ANY] * 4,
        out_specs=(ANY,) * 4,
        scratch_shapes=[
            vm((4, 2, tokens, width), bf),
            vm((4, 2, tokens, width), bf),
            vm(wgu_all.shape, bf),
            vm(wd_all.shape, bf),
            vm((4, 2 * tokens, FF_PAD), f32),
            vm((4, 2 * tokens, FF_PAD), bf),
            vm((4, 2 * tokens, 2 * FF_PAD), bf),
            vm((4, 2, tokens, width), bf),
            vm((4, 2, tokens, width), bf),
            vm((2, tokens, width), f32),
            vm(wgu_all.shape, bf),
        ]
        + sums
        + sums
        + [
            pltpu.SemaphoreType.DMA((8,)),
            pltpu.SemaphoreType.DMA((32,)),
            pltpu.SemaphoreType.DMA((32,)),
        ],
        compiler_params=comm_params(2),
        name="feed_forward",
    )(own_n, gb_all, wgu_all, wd_all)


def reduce_kernel(
    dgu, dd, dqkv, dwo, dgain,
    o_gu, o_d, o_qkv, o_wo, o_gain,
    h_gu, r_gu, f_gu, h_d, r_d, h_qkv, r_qkv, h_wo, r_wo, h_gain, r_gain,
    y_gu, y_d, y_qkv, y_wo, y_gain, p_gu, p_d, p_qkv, p_wo, p_gain, z_gu, z_d, z_qkv, z_wo, z_gain,
    qa, qb, qm, qp, qz, wa, wb, wm, wp, wz, ga, gb_, gm, gp, gz,
    local_sems, send_sems, recv_sems,
):
    place = Place()
    wire = Wire(send_sems, recv_sems)
    core, me, y = place.core, place.shard, place.y
    others = [(j, p) for p in (0, 1) for j in range(4) if (j, p) != (0, 0)]
    group = [place.device(dx=STEPS[j], mirror=p) for j, p in others]
    sibling = place.device(sibling=1)
    column = [place.device(dy=d) for d in (1, 3, 2)]
    low = place.device(swap_lo=1)

    def lanes(ref, which, size):
        start = pl.multiple_of(which * size, 128)
        return ref.at[..., pl.ds(start, size)]

    def gu_half(ref, which):
        return ref.at[:, :, pl.ds(pl.multiple_of(which * FF_PAD, 128), FF_PAD)]

    def d_half(ref, which):
        return ref.at[pl.ds(pl.multiple_of(which * 448, 16), 448)]

    def qkv_half(ref, which):
        return ref.at[:, :, pl.ds(pl.multiple_of(which * 768, 128), 768)]

    def wo_half(ref, which):
        return ref.at[:, pl.ds(pl.multiple_of(which * 64, 16), 64)]

    locals_ = []

    def local(src, dst):
        copy = pltpu.make_async_copy(src, dst, local_sems.at[len(locals_)])
        copy.start()
        locals_.append(copy)
        return copy

    mine = [
        local(gu_half(dgu, core), h_gu),
        local(d_half(dd, core), h_d),
        local(qkv_half(dqkv, core), h_qkv),
        local(wo_half(dwo, core), h_wo),
        local(dgain, h_gain),
    ]
    greet([sibling, low] + group + column)
    swaps = [
        wire.copy(gu_half(dgu, 1 - core), r_gu, sibling),
        wire.copy(qkv_half(dqkv, 1 - core), r_qkv, sibling),
        wire.copy(wo_half(dwo, 1 - core), r_wo, sibling),
        wire.copy(dgain, r_gain, sibling),
        wire.copy(d_half(dd, 1 - core), r_d, sibling),
    ]
    for swap in swaps:
        swap.start()
    for copy in mine:
        copy.wait()

    def summed(target, source, count):
        def one(i, carry):
            add_into(target.at[i], source.at[i])
            return carry

        lax.fori_loop(0, count, one, 0)

    swaps[0].wait_recv()
    summed(h_gu, r_gu, 8)
    swaps[0].wait_send()
    turn = [
        wire.copy(h_gu.at[place.shard_at(j, p)], f_gu.at[me], device)
        for (j, p), device in zip(others, group)
    ]
    for copy in turn:
        copy.start()
    f_gu[me] = h_gu[me]
    for swap in swaps[1:4]:
        swap.wait_recv()
    summed(h_qkv, r_qkv, 8)
    summed(h_wo, r_wo, 8)
    summed(h_gain, r_gain, 8)

    def cut_lanes(size):
        def cut(ref, part):
            return ref if part == 0 else ref.at[:, pl.ds((part - 1) * size, size)]

        return cut

    def cut_rows(size):
        def cut(ref, part):
            return ref if part == 0 else ref.at[pl.ds((part - 1) * size, size)]

        return cut

    at = place.shard_at
    sums = [
        SumTree(wire, place, lambda j, p: h_qkv.at[at(j, p)], cut_lanes(384), qa, qb, qm, qp, qz),
        SumTree(wire, place, lambda j, p: h_wo.at[at(j, p)], cut_rows(32), wa, wb, wm, wp, wz),
        SumTree(wire, place, lambda j, p: h_gain.at[at(j, p)], cut_lanes(128), ga, gb_, gm, gp, gz),
    ]
    for tree in sums:
        tree.send_far()
    swaps[4].wait_recv()
    add_into(h_d, r_d)

    def quarter_gu(ref, which):
        return ref.at[pl.ds(which * 2, 2)]

    def quarter_d(ref, which):
        return ref.at[pl.ds(pl.multiple_of(which * 112, 16), 112)]

    steps = (1, 3, 2)
    over_d = [
        wire.copy(quarter_d(h_d, (y + d) % 4), y_d.at[y], device)
        for d, device in zip(steps, column)
    ]
    for copy in over_d:
        copy.start()
    for tree in sums:
        tree.send_near()
    for copy in turn:
        copy.wait_recv()
    over_gu = [
        wire.copy(quarter_gu(f_gu, (y + d) % 4), y_gu.at[y], device)
        for d, device in zip(steps, column)
    ]
    for copy in over_gu:
        copy.start()
    y_gu[y] = quarter_gu(f_gu, y)[...]
    y_d[y] = quarter_d(h_d, y)[...]
    for tree in sums:
        tree.send_last()
    for tree, target in zip(sums, (y_qkv, y_wo, y_gain)):
        target[y] = tree.finish().astype(jnp.bfloat16)
    over_small = [
        [wire.copy(target.at[y], target.at[y], device) for device in column]
        for target in (y_qkv, y_wo, y_gain)
    ]
    for copies in over_small:
        for copy in copies:
            copy.start()

    def add_up(source):
        return (
            source[0].astype(jnp.float32)
            + source[1].astype(jnp.float32)
            + source[2].astype(jnp.float32)
            + source[3].astype(jnp.float32)
        )

    def across(copies, source, piece, other):
        for copy in copies:
            copy.wait_recv()
        piece[...] = add_up(source).astype(jnp.bfloat16)
        made = wire.copy(piece, other, low)
        made.start()
        return made

    crossings = [
        across(over_d, y_d, p_d, z_d),
        across(over_gu, y_gu, p_gu, z_gu),
        across(over_small[0], y_qkv, p_qkv, z_qkv),
        across(over_small[1], y_wo, p_wo, z_wo),
        across(over_small[2], y_gain, p_gain, z_gain),
    ]

    def settle(crossing, piece, other):
        crossing.wait_recv()
        crossing.wait_send()
        add_into(piece, other)

    def out_gu(which, half):
        return o_gu.at[
            pl.ds(which * 2, 2), :, pl.ds(pl.multiple_of(half * FF_PAD, 128), FF_PAD)
        ]

    def out_d(which, half):
        return o_d.at[pl.ds(pl.multiple_of(half * 448 + which * 112, 16), 112)]

    ends = []
    settle(crossings[0], p_d, z_d)
    back_d = [wire.copy(p_d, out_d(y, core), device) for device in column]
    ends.append(wire.copy(p_d, out_d(y, core), sibling))
    for copy in back_d + ends[-1:]:
        copy.start()
    local(p_d, out_d(y, core))
    settle(crossings[1], p_gu, z_gu)
    back_gu = [wire.copy(p_gu, out_gu(y, core), device) for device in column]
    ends.append(wire.copy(p_gu, out_gu(y, core), sibling))
    for copy in back_gu + ends[-1:]:
        copy.start()
    local(p_gu, out_gu(y, core))
    out_qkv = o_qkv.at[:, pl.ds(pl.multiple_of(core * 768, 128), 768)]
    out_wo = o_wo.at[pl.ds(pl.multiple_of(core * 64, 16), 64)]
    for crossing, piece, other, out in (
        (crossings[2], p_qkv, z_qkv, out_qkv),
        (crossings[3], p_wo, z_wo, out_wo),
    ):
        settle(crossing, piece, other)
        ends.append(wire.copy(piece, out, sibling))
        ends[-1].start()
        local(piece, out)
    settle(crossings[4], p_gain, z_gain)
    local(p_gain, o_gain)
    for backs, out in ((back_d, out_d), (back_gu, out_gu)):
        for d, copy in zip((3, 1, 2), backs):
            copy.wait_recv()
            which = (y + d) % 4
            ends.append(wire.copy(out(which, core), out(which, core), sibling))
            ends[-1].start()
    for copy in ends:
        copy.wait_recv()
    for copy in locals_[5:]:
        copy.wait()
    waited = [id(made) for made in swaps[:1] + crossings]
    for made in wire.made:
        if id(made) not in waited:
            made.wait_send()


def reduce_all(dgu, dd, dqkv, dwo, dgain):
    bf = jnp.bfloat16
    vm = lambda *s: pltpu.VMEM(s, bf)
    shape = lambda *s: jax.ShapeDtypeStruct(s, bf)
    h_gu, h_qkv, h_wo, h_gain, h_d = (8, 144, 896), (8, 144, 768), (8, 64, 1152), (8, 16, 256), (448, 1152)
    q_gu, q_d = (2, 144, 896), (112, 1152)
    unit = [h_qkv[1:], h_wo[1:], h_gain[1:]]
    halves = [(144, 384), (32, 1152), (16, 128)]
    trees = []
    for whole, half in zip(unit, halves):
        trees += [vm(2, *half), vm(2, *half), vm(2, *whole), vm(2, *whole), vm(*whole)]
    return pl.pallas_call(
        reduce_kernel,
        out_shape=(shape(8, 144, 1792), shape(896, 1152), shape(144, 1536), shape(128, 1152), shape(16, 256)),
        in_specs=[ANY] * 5,
        out_specs=(ANY,) * 5,
        scratch_shapes=[
            vm(*h_gu), vm(*h_gu), vm(*h_gu), vm(*h_d), vm(*h_d), vm(*h_qkv), vm(*h_qkv),
            vm(*h_wo), vm(*h_wo), vm(*h_gain), vm(*h_gain),
        ]
        + [vm(4, *s) for s in (q_gu, q_d, *unit)]
        + [vm(*s) for s in (q_gu, q_d, *unit)]
        + [vm(*s) for s in (q_gu, q_d, *unit)]
        + trees
        + [
            pltpu.SemaphoreType.DMA((12,)),
            pltpu.SemaphoreType.DMA((96,)),
            pltpu.SemaphoreType.DMA((96,)),
        ],
        compiler_params=comm_params(5),
        name="reduce_grads",
    )(dgu, dd, dqkv, dwo, dgain)


def rotate(vectors, cosine, sine_part):
    half_size = vectors.shape[-1] // 2
    first_half = vectors[..., :half_size]
    second_half = vectors[..., half_size:]
    return jnp.concatenate(
        [
            first_half * cosine - second_half * sine_part,
            second_half * cosine + first_half * sine_part,
        ],
        axis=-1,
    )


def norm_back(grad_normed, scaled, inverse, gain_values):
    grad_scaled = grad_normed * gain_values
    return inverse * (grad_scaled - scaled * jnp.mean(grad_scaled * scaled, axis=1, keepdims=True))


def pack_gate_up(w_gate, w_up):
    rows = w_gate.shape[0]

    def cut(weight):
        parts = weight.reshape(rows, 8, FF_DEV)
        return jnp.pad(parts, ((0, 0), (0, 0), (0, FF_PAD - FF_DEV))).reshape(rows, 8, PAIRS, 128)

    both = jnp.stack([cut(w_gate), cut(w_up)], axis=3)
    return both.transpose(1, 0, 2, 3, 4).reshape(8, rows, 2 * FF_PAD)


def unpack_gate_up(both):
    rows = both.shape[1]
    split = both.reshape(8, rows, PAIRS, 2, 128)

    def join(k):
        parts = split[:, :, :, k].reshape(8, rows, FF_PAD)[:, :, :FF_DEV]
        return parts.transpose(1, 0, 2).reshape(rows, 8 * FF_DEV).astype(jnp.float32)

    return join(0), join(1)


def gain_rows(*rows):
    made = jnp.stack([jnp.pad(row, ((0, 0), (0, 256 - row.shape[1]))) for row in rows], axis=1)
    return jnp.pad(made, ((0, 0), (0, 16 - len(rows)), (0, 0))).astype(jnp.bfloat16)


def on_device(
    tokens, lengths, attn_gain, w_query, w_keyval, w_out, mlp_gain, w_gate, w_up, w_down, cotangent
):
    row_count, width = tokens.shape
    head_size = w_keyval.shape[1] // 2
    heads_all = w_query.shape[1]
    head_count = heads_all // head_size
    scaling = head_size ** (-0.5)
    shard = lax.axis_index("shard")
    within = jnp.arange(row_count, dtype=jnp.int32)
    live_count = lengths[0, 0]
    keep_mask = (within < live_count).astype(jnp.float32)[:, None]
    grad_out = cotangent.astype(jnp.float32)
    grad_branch = (keep_mask * grad_out).astype(jnp.bfloat16)

    counts = jnp.full((1, 144), live_count, jnp.int32).astype(jnp.bfloat16)
    misc = gain_rows(attn_gain[None], mlp_gain[None], counts)[0]
    miscs, qkv_all, out_all, gu_all, branch_all = spread(
        misc,
        jnp.concatenate([w_query, w_keyval], axis=1),
        w_out,
        pack_gate_up(w_gate, w_up),
        grad_branch,
    )
    gain1 = miscs[:, 0, :144].reshape(width).astype(jnp.float32)
    gain2 = miscs[:, 1, :144].reshape(width).astype(jnp.float32)
    live_all = miscs[:, 2, 0].astype(jnp.int32)
    qkv_full = qkv_all.reshape(width, -1)
    out_full = out_all.reshape(heads_all, width)
    down_mine = jnp.pad(w_down, ((0, FF_PAD - FF_DEV), (0, 0)))

    starts = jnp.cumsum(live_all) - live_all
    offset = starts[shard]
    query_pos = offset + within
    back = shard - jnp.arange(BEHIND + 1)
    back_start = jnp.where(back >= 0, starts[jnp.maximum(back, 0)], 0)
    back_live = jnp.where(back >= 0, live_all[jnp.maximum(back, 0)], 0)
    key_pos = (back_start[:, None] + within[None]).reshape(-1)
    key_live = (within[None] < back_live[:, None]).reshape(-1)
    allowed = (
        key_live[None, :]
        & (key_pos[None, :] <= query_pos[:, None])
        & (query_pos[:, None] - key_pos[None, :] < WINDOW)
    )
    half_size = head_size // 2
    frequency = 10000.0 ** (-2.0 * jnp.arange(half_size, dtype=jnp.float32) / head_size)
    angles = query_pos.astype(jnp.float32)[:, None] * frequency[None, :]
    cosine = jnp.cos(angles)
    sine_part = jnp.sin(angles)
    heads_cos = cosine[:, None, :]
    heads_sin = sine_part[:, None, :]
    inputs = tokens.astype(jnp.float32)
    inverse1 = lax.rsqrt(jnp.mean(inputs * inputs, axis=1, keepdims=True) + EPSILON)
    scaled1 = inputs * inverse1
    normed1 = (scaled1 * gain1).astype(jnp.bfloat16)
    projected = matmul(normed1, qkv_full)
    queries = (
        rotate(
            projected[:, :heads_all].reshape(row_count, head_count, head_size),
            heads_cos,
            heads_sin,
        )
        * scaling
    ).astype(jnp.bfloat16)
    own_keys = rotate(
        projected[:, heads_all : heads_all + head_size], cosine, sine_part
    ).astype(jnp.bfloat16)
    own_values = projected[:, heads_all + head_size :].astype(jnp.bfloat16)
    own_kv = jnp.concatenate([own_keys, own_values], axis=1)
    behind = window(own_kv, False, 3, "keys_values")
    behind = jnp.where((back[1:] >= 0)[:, None, None], behind, 0)
    all_kv = jnp.concatenate([own_kv[None], behind], axis=0).reshape(-1, 2 * head_size)
    keys, values = all_kv[:, :head_size], all_kv[:, head_size:]

    raw_scores = jnp.einsum("thd,gd->htg", queries, keys, preferred_element_type=jnp.float32)
    scores = jnp.where(allowed[None], raw_scores, MASKED)
    row_max = jnp.max(scores, axis=-1, keepdims=True)
    raised = jnp.exp(scores - row_max)
    probs = raised / jnp.sum(raised, axis=-1, keepdims=True)
    probs_low = probs.astype(jnp.bfloat16)
    attended = jnp.einsum("htg,gd->thd", probs_low, values, preferred_element_type=jnp.float32)
    attended = attended.reshape(row_count, heads_all).astype(jnp.bfloat16)
    middle = inputs + keep_mask * matmul(attended, out_full)
    inverse2 = lax.rsqrt(jnp.mean(middle * middle, axis=1, keepdims=True) + EPSILON)
    scaled2 = middle * inverse2
    normed2 = (scaled2 * gain2).astype(jnp.bfloat16)

    grad_normed2, branch, grad_gu, grad_d = feed_forward(
        normed2, branch_all, gu_all.reshape(width, -1), down_mine
    )
    outputs = (middle + keep_mask * branch).astype(jnp.bfloat16)
    grad_gain2 = jnp.sum(grad_normed2 * scaled2, axis=0)
    grad_middle = grad_out + norm_back(grad_normed2, scaled2, inverse2, gain2)

    grad_attn = (keep_mask * grad_middle).astype(jnp.bfloat16)
    grad_out_w = lead_product(attended, grad_attn)
    grad_attended = (
        trail_product(grad_attn, out_full)
        .astype(jnp.bfloat16)
        .reshape(row_count, head_count, head_size)
    )
    grad_probs = jnp.einsum(
        "thd,gd->htg", grad_attended, values, preferred_element_type=jnp.float32
    )
    grad_values_all = jnp.einsum(
        "htg,thd->gd", probs_low, grad_attended, preferred_element_type=jnp.float32
    )
    row_delta = jnp.sum(probs * grad_probs, axis=-1, keepdims=True)
    grad_scores = (probs * (grad_probs - row_delta)).astype(jnp.bfloat16)
    grad_queries = jnp.einsum("htg,gd->thd", grad_scores, keys, preferred_element_type=jnp.float32)
    grad_keys_all = jnp.einsum(
        "htg,thd->gd", grad_scores, queries, preferred_element_type=jnp.float32
    )
    grad_kv_all = jnp.concatenate([grad_keys_all, grad_values_all], axis=1)
    grad_kv_all = grad_kv_all.reshape(BEHIND + 1, row_count, 2 * head_size)
    ahead = window(grad_kv_all.astype(jnp.bfloat16), True, 4, "grad_keys_values")
    is_ahead = (shard + 1 + jnp.arange(BEHIND) < 8)[:, None, None]
    grad_own_kv = grad_kv_all[0] + jnp.sum(
        jnp.where(is_ahead, ahead, 0).astype(jnp.float32), axis=0
    )
    grad_query_proj = (
        (rotate(grad_queries, heads_cos, -heads_sin) * scaling)
        .reshape(row_count, heads_all)
        .astype(jnp.bfloat16)
    )
    grad_keyval_proj = jnp.concatenate(
        [
            rotate(grad_own_kv[:, :head_size], cosine, -sine_part),
            grad_own_kv[:, head_size:],
        ],
        axis=1,
    ).astype(jnp.bfloat16)
    grad_proj = jnp.concatenate([grad_query_proj, grad_keyval_proj], axis=1)
    grad_qkv_w = lead_product(normed1, grad_proj)
    grad_normed1 = trail_product(grad_proj, qkv_full)
    grad_gain1 = jnp.sum(grad_normed1 * scaled1, axis=0)
    grad_inputs = grad_middle + norm_back(grad_normed1, scaled1, inverse1, gain1)

    sum_gu, sum_d, sum_qkv, sum_wo, sum_gain = reduce_all(
        grad_gu.reshape(8, 144, -1),
        grad_d,
        grad_qkv_w.astype(jnp.bfloat16).reshape(8, 144, -1),
        grad_out_w.astype(jnp.bfloat16).reshape(8, 128, width),
        gain_rows(grad_gain1.reshape(8, 144), grad_gain2.reshape(8, 144)),
    )
    grad_gate_w, grad_up_w = unpack_gate_up(sum_gu)
    sum_qkv = sum_qkv.astype(jnp.float32)
    return (
        outputs,
        grad_inputs,
        sum_gain[0, :144].astype(jnp.float32),
        sum_qkv[:, :heads_all],
        sum_qkv[:, heads_all:],
        sum_wo.astype(jnp.float32),
        sum_gain[1, :144].astype(jnp.float32),
        grad_gate_w,
        grad_up_w,
        sum_d[:FF_DEV].astype(jnp.float32),
    )


def solution(mesh):
    placed = (
        P(("rep", "shard"), None),
        P("rep", "shard"),
        P("shard"),
        P("shard", None),
        P("shard", None),
        P("shard", None),
        P("shard"),
        P("shard", None),
        P("shard", None),
        P("shard", None),
        P(("rep", "shard"), None),
    )
    return jax.shard_map(
        on_device,
        mesh=mesh,
        in_specs=placed,
        out_specs=(
            P(("rep", "shard"), None),
            P(("rep", "shard"), None),
            P("shard"),
            P("shard", None),
            P("shard", None),
            P("shard", None),
            P("shard"),
            P("shard", None),
            P("shard", None),
            P("shard", None),
        ),
        check_vma=False,
    )
```

time: 1940 us -> 525 us (0.27)
  waiting for transfers between devices: 1590 us -> 0 us
  Pallas kernels: 0 us -> 361 us
  blocking collectives: 146 us -> 0 us
  matrix products: 139 us -> 17.4 us
  local copies, waits for them, and re-layouts: 6.56 us -> 102 us
    reduce_scatter x8 -> x0, waiting for transfers between devices: 926 us -> none  [the longest x1 200 us: on_device(): lax.psum_scatter(grad_gate_w.astype(jnp.bfloat16), 'shard', scatter_dimen...]
    all_gather x6 -> x0, waiting for transfers between devices: 558 us -> none  [the longest x1 177 us: on_device(): lax.all_gather(w_up, 'shard', axis=0, tiled=True)]
    pallas_call x0 -> x5, Pallas kernels: none -> 361 us  [the longest x1 136 us: reduce_all(): pl.pallas_call(reduce_kernel, out_shape=(shape(8, 144, 1792), shape(896,...]
    psum x1 -> x0, waiting for transfers between devices: 104 us -> none  [on_device(): lax.psum(attn_grads[1].astype(jnp.bfloat16), 'rep').astype(jnp.float32)]
    all_gather x2 -> x0, blocking collectives: 63.9 us -> none  [the longest x1 32.4 us: on_device(): lax.all_gather(own_keys, 'shard', axis=0, tiled=True)]
    dot_general x6 -> x2, matrix products: 43 us -> 4.17 us  [trail_product(): lax.dot_general(former, latter, (((1,), (1,)), ((), ())), preferred_eleme...]
    dot_general x6 -> x2, matrix products: 42.4 us -> 3.8 us  [matmul(): return jnp.dot(former, latter, preferred_element_type=jnp.float32)]
    unnamed x2 -> x0, blocking collectives: 37.3 us -> none
  transfers between devices with their start and end apart: 15 -> 0, of which waited for: 14 -> 0; matrix products, arithmetic and copies ran while one was open for 6% -> 0% of each run, Pallas kernels for 0% -> 0%
where the time goes in v1:
time: 525 us; the launch traced here: 516 us
  Pallas kernels  361 us (69%)
  local copies, waits for them, and re-layouts  102 us (19%)
  other arithmetic  34 us (6%)
  matrix products  17.4 us (3%)
    pallas_call x1, Pallas kernels, reduce_all(): pl.pallas_call(reduce_kernel, out_shape=(shape(8, 144, 1792), shape(896,...  136 us
    pallas_call x1, Pallas kernels, feed_forward(): pl.pallas_call(ff_kernel, out_shape=(jax.ShapeDtypeStruct((tokens, width)...  108 us
    pallas_call x1, Pallas kernels, spread(): pl.pallas_call(spread_kernel, out_shape=(shape(8, *misc.shape), shape(8,...  88.3 us
    pallas_call x2, Pallas kernels, window(): pl.pallas_call(functools.partial(window_kernel, reverse), out_shape=jax.S...  28.2 us
    slice x1, local copies, waits for them, and re-layouts, join(): parts = split[:, :, :, k].reshape(8, rows, FF_PAD)[:, :, :FF_DEV]  25.8 us
    convert_element_type x4, local copies, waits for them, and re-layouts, join(): parts.transpose(1, 0, 2).reshape(rows, 8 * FF_DEV).astype(jnp.float32)  16.8 us
    reshape x2, local copies, waits for them, and re-layouts, cut(): parts = weight.reshape(rows, 8, FF_DEV)  10.8 us

profile of v1, /device:TPU:1, one launch (start us, length us, event | category | flops | bytes accessed | tf_op | source)
XLA Modules:
  0.0 515.9 jit_solution(17491341167889046653)
XLA Ops:
  2.8 1.2 fusion.21
  4.6 1.9 fusion.14.gb
  6.5 1.8 pad_maximum_fusion.3.qkv
  8.4 4.9 reshape.379
  13.3 5.8 %reshape.380 = bf16[144,8,864]{2,1,0:T(8,128)(2,1)} reshape(bf16[144,6912]{1,0:T(8,128)(2,1)} %param.19) | data formatting | bytes 3981312 | tf_op jit(solution)/shard_map/reshape | solution.py:829
  19.1 2.3 pad_bitcast_fusion
  22.1 5.1 copy.40
  27.3 10.3 %reshape.381.gu = bf16[8,144,1792]{2,1,0:T(8,128)(2,1)} reshape(bf16[8,144,7,2,128]{4,3,2,1,0:T(2,128)(2,1)} %copy.40) | data formatting | bytes 8257536 | tf_op jit(solution)/shard_map/reshape | solution.py:833
  37.5 1.5 pad.45.wd_all
  39.0 88.3 %spread_weights.1 = (bf16[8,16,256]{2,1,0:T(8,128)(2,1)}, bf16[8,144,1536]{2,1,0:T(8,128)(2,1)}, bf16[8,128,1152]{2,1,0:T(8,128)(2,1)}, bf16[8,144,1792]{2,1,0:T(8,128)(2,1)}, bf16[4,2,192,1152]{3,2,1,0:T(8,128)(2,1)}) custom-call(bf16[16,256]{1,0:T(8,128)(2,1)} %fusion.65.misc, bf16[144,1536]{1,0:T(8,128)(2,1)} %pad_maximum_fusion.3.qkv, ...), custom_call_target="tpu_custom_call" | custom-call | tf_op jit(solution)/shard_map/spread_weights/pallas_call | solution.py:229
  127.3 1.0 convert_reduce_fusion.3
  128.3 0.9 convert_reduce_fusion.1
  133.4 3.0 fusion.43
  138.4 17.0 %keys_values.1 = bf16[4,192,512]{2,1,0:T(8,128)(2,1)} custom-call(bf16[192,512]{1,0:T(8,128)(2,1)} %get-tuple-element.59.own), custom_call_target="tpu_custom_call" | custom-call | tf_op jit(solution)/shard_map/keys_values/pallas_call | solution.py:291
  155.4 1.3 broadcast_select_fusion
  157.3 1.4 fusion.76
  159.4 1.0 copy-done
  160.5 1.2 copy-done.2
  161.7 0.8 multiply_reduce_fusion.2
  162.6 0.9 multiply_convert_fusion.1.own_n
  163.5 108.1 %feed_forward.1 = (f32[192,1152]{1,0:T(8,128)}, f32[192,1152]{1,0:T(8,128)}, bf16[1152,1792]{1,0:T(8,128)(2,1)}, bf16[896,1152]{1,0:T(8,128)(2,1)}) custom-call(bf16[192,1152]{1,0:T(8,128)(2,1)} %multiply_convert_fusion.1.own_n, bf16[4,2,192,1152]{3,2,1,0:T(8,128)(2,1)} %get-tuple-element.27.gb_all, bf16[1152,1792]{1,0:T(8,128)(2,1)} %bitcast.105, ...), custom_call_target="tpu_custom_call" | custom-call | tf_op jit(solution)/shard_map/feed_forward/pallas_call | solution.py:516
  271.6 1.5 multiply_reduce_fusion
  273.2 2.7 convert_add_fusion
  275.9 2.8 convolution_convert_fusion.2
  278.7 0.9 convolution_bitcast_fusion
  279.7 2.3 convolution_convert_fusion.1
  286.0 1.0 fusion.6
  287.1 11.2 %grad_keys_values.1 = bf16[4,192,512]{2,1,0:T(8,128)(2,1)} custom-call(bf16[5,192,512]{2,1,0:T(8,128)(2,1)} %bitcast.106), custom_call_target="tpu_custom_call" | custom-call | tf_op jit(solution)/shard_map/grad_keys_values/pallas_call | solution.py:291
  298.3 1.6 convert_reduce_fusion
  300.5 1.4 fusion.20
  302.1 1.2 fusion.19
  303.9 3.0 convolution_convert_fusion
  306.9 135.9 %reduce_grads.1 = (bf16[8,144,1792]{2,1,0:T(8,128)(2,1)}, bf16[896,1152]{1,0:T(8,128)(2,1)}, bf16[144,1536]{1,0:T(8,128)(2,1)}, bf16[128,1152]{1,0:T(8,128)(2,1)}, bf16[16,256]{1,0:T(8,128)(2,1)}) custom-call(bf16[8,144,1792]{2,1,0:T(8,128)(2,1)} %bitcast.104, bf16[896,1152]{1,0:T(8,128)(2,1)} %get-tuple-element.32.dd, bf16[8,144,1536]{2,1,0:T(8,128)(2,1)} %bitcast.111, ...), custom_call_target="tpu_custom_call" | custom-call | tf_op jit(solution)/shard_map/reduce_grads/pallas_call | solution.py:784
  442.8 1.4 slice_convert_fusion.3
  444.2 1.7 slice.137
  445.9 1.8 slice.136
  447.7 1.8 convert_element_type.217
  449.5 2.2 slice_convert_fusion
  451.7 8.6 %reshape.394 = bf16[8,144,7,2,128]{4,3,2,1,0:T(2,128)(2,1)} reshape(bf16[8,144,1792]{2,1,0:T(8,128)(2,1)} %get-tuple-element.36) | data formatting | bytes 8257536 | tf_op jit(solution)/shard_map/reshape | solution.py:838
  460.3 25.8 %slice_reduce_fusion = (bf16[8,144,7,128]{3,2,1,0:T(8,128)(2,1)}, bf16[8,144,7,128]{3,2,1,0:T(8,128)(2,1)S(1)}) fusion(bf16[8,144,7,2,128]{4,3,2,1,0:T(2,128)(2,1)} %reshape.394), kind=kLoop, calls=%fused_computation.4 | loop fusion | bytes 8257536 | tf_op jit(solution)/shard_map/slice | solution.py:841
  486.2 5.1 reshape_squeeze.9
  491.3 1.8 convert_bitcast_fusion
  493.1 3.2 copy.52
  496.3 5.2 %reshape.402 = f32[144,6912]{1,0:T(8,128)} reshape(f32[144,8,864]{2,1,0:T(8,128)} %copy.52) | data formatting | bytes 7962624 | tf_op jit(solution)/shard_map/convert_element_type | solution.py:842
  501.6 3.6 reshape_squeeze.8
  505.2 1.8 convert_bitcast_fusion.1
  507.0 3.2 copy.50
  510.2 5.2 %reshape.401 = f32[144,6912]{1,0:T(8,128)} reshape(f32[144,8,864]{2,1,0:T(8,128)} %copy.50) | data formatting | bytes 7962624 | tf_op jit(solution)/shard_map/convert_element_type | solution.py:842
  (91 shorter events, 15.9 us)
Async XLA Ops:
  27.2 10.3 %copy-start.7 = (bf16[864,1152]{1,0:T(8,128)(2,1)S(1)}, bf16[864,1152]{1,0:T(8,128)(2,1)}, u32[]{:S(2)}) copy-start(bf16[864,1152]{1,0:T(8,128)(2,1)} %param.20) | copy-start | bytes 5971972
  39.0 94.4 %copy-start.3 = (bf16[192,1152]{1,0:T(8,128)(2,1)S(1)}, bf16[192,1152]{1,0:T(8,128)(2,1)}, u32[]{:S(2)}) copy-start(bf16[192,1152]{1,0:T(8,128)(2,1)} %param.11) | copy-start | bytes 1327108
  137.5 19.2 %copy-start.9 = (f32[192,4,128]{2,0,1:T(8,128)}, f32[192,4,128]{2,0,1:T(8,128)S(1)}, u32[]{:S(2)}) copy-start(f32[192,4,128]{2,0,1:T(8,128)S(1)} %get-tuple-element.50) | copy-start | bytes 1179652
  137.5 19.2 %copy-start.11 = (f32[192,4,128]{2,0,1:T(8,128)}, f32[192,4,128]{2,0,1:T(8,128)S(1)}, u32[]{:S(2)}) copy-start(f32[192,4,128]{2,0,1:T(8,128)S(1)} %get-tuple-element.51) | copy-start | bytes 1179652
  158.8 1.7 copy-start
  158.8 2.9 copy-start.2
  160.5 3.0 copy-start.4
  275.9 2.8 copy-start.1
  278.7 1.0 copy-start.5
  283.3 1.0 copy-start.10
  283.3 1.1 copy-start.12
  298.2 2.2 copy-start.6
  298.3 2.3 copy-start.13
  302.0 2.0 copy-start.14
  442.8 6.7 %copy-start.8 = (bf16[896,1152]{1,0:T(8,128)(2,1)S(1)}, bf16[896,1152]{1,0:T(8,128)(2,1)}, u32[]{:S(2)}) copy-start(bf16[896,1152]{1,0:T(8,128)(2,1)} %get-tuple-element.37) | copy-start | bytes 6193156
